TPU v7x, 32 devices: a whole 2x2x4 slice. The times are simulated.
32 devices in a mesh: groups: 2 (over y), row: 2 (over core), col: 8 (over z, x).
Axes of the slice: x: 2, y: 2, z: 4, core: 2. Of those that a mesh axis runs over, the one named last changes fastest.
Arguments:
- inputs: bfloat16 [512, 2, 6144], P(('groups', 'row'), None, 'col'), parts along dimension 0, may hold values from -6 to 6
- weights: bfloat16 [12288, 24576], P('row', 'col'), may hold values from -0.0546875 to 0.0546875
- grad_act: bfloat16 [512, 24576], P(('groups', 'row'), 'col'), parts along dimension 0, may hold values from -6 to 6
Outputs:
- activation: bfloat16 [512, 24576], P(('groups', 'row'), 'col'), parts along dimension 0
- grad_x: bfloat16 [512, 2, 6144], P(('groups', 'row'), None, 'col'), parts along dimension 0
- grad_w: bfloat16 [24576, 24576], P(('groups', 'row'), 'col'), parts along dimension 0
There are 2 independent parts, one for each index of `groups`. A program takes and returns all parts, laid end to end along the dimension named above; an argument that names none is the same for every part. Nothing has to cross between parts.
All inputs are finite; a program needn't handle non-finite values.
Results may differ from a plain program's by a relative error of at most 0.0049.
Values may be sent and summed in bfloat16 or wider, within the bound.
A program may use at most 448 MiB of HBM per device.

v0:
```python
import math

import jax
import jax.numpy as jnp
from jax import lax
from jax.sharding import PartitionSpec as P

root_coef = math.sqrt(2.0 / math.pi)
cube_coef = 0.044715


def tanh_gelu(preact):
    tanh_arg = root_coef * (preact + cube_coef * preact * preact * preact)
    return 0.5 * preact * (1.0 + jnp.tanh(tanh_arg))


def gelu_slope(preact):
    tanh_arg = root_coef * (preact + cube_coef * preact * preact * preact)
    tangent = jnp.tanh(tanh_arg)
    return 0.5 * (1.0 + tangent) + 0.5 * preact * (1.0 - tangent * tangent) * root_coef * (
        1.0 + 3.0 * cube_coef * preact * preact
    )


def local(inputs, weights, grad_act):
    tok_rows, row_count, piece_cols = inputs.shape
    half_rows, hid_cols = weights.shape
    all_tokens = tok_rows * row_count
    col_count = lax.axis_size("col")
    features = lax.all_gather(inputs, "col", axis=2, tiled=True)
    weight_cols = lax.all_gather(weights, "row", axis=0, tiled=True)
    preact = jnp.dot(
        features.reshape(tok_rows, row_count * half_rows),
        weight_cols,
        preferred_element_type=jnp.float32,
    )
    own_half = lax.all_to_all(features, "row", split_axis=1, concat_axis=0, tiled=True).reshape(
        all_tokens, half_rows
    )
    activation = tanh_gelu(preact).astype(jnp.bfloat16)
    grad_pre = (grad_act.astype(jnp.float32) * gelu_slope(preact)).astype(jnp.bfloat16)
    grad_all = lax.all_gather(grad_pre, "row", axis=0, tiled=True)
    grad_w = lax.dot_general(
        own_half, grad_all, (((0,), (0,)), ((), ())), preferred_element_type=jnp.float32
    ).astype(jnp.bfloat16)
    local_terms = lax.dot_general(
        grad_all, weights, (((1,), (1,)), ((), ())), preferred_element_type=jnp.float32
    )
    split_terms = local_terms.reshape(all_tokens, col_count, piece_cols)
    received = lax.all_to_all(split_terms, "col", split_axis=1, concat_axis=1, tiled=True)
    summed = jnp.sum(received, axis=1).astype(jnp.bfloat16)
    arranged = summed.reshape(row_count, tok_rows, 1, piece_cols)
    moved = lax.all_to_all(arranged, "row", split_axis=0, concat_axis=2, tiled=True)
    grad_x = moved.reshape(tok_rows, row_count, piece_cols)
    return (activation, grad_x, grad_w)


def solution(mesh):
    placed = (P(("groups", "row"), None, "col"), P("row", "col"), P(("groups", "row"), "col"))
    return jax.shard_map(
        local,
        mesh=mesh,
        in_specs=placed,
        out_specs=(
            P(("groups", "row"), "col"),
            P(("groups", "row"), None, "col"),
            P(("groups", "row"), "col"),
        ),
        check_vma=False,
    )
```

profile of v0, /device:TPU:0, one launch (start us, length us, event | category | flops | bytes accessed | tf_op | source)
XLA Modules:
  0.0 404.7 jit_solution(8034229897867743177)
XLA Ops:
  7.2 0.0 all-gather.4.cloned.1.call-start
  7.2 1.9 copy.14
  9.1 0.0 all-gather.4.cloned.1.call-update
  9.2 0.0 copy-start
  9.2 0.0 all-gather.6.cloned.1.call-start
  9.2 0.7 all-gather.6.cloned.1.call-update
  9.9 0.0 all-gather.8.cloned.1.call-start
  10.0 64.0 %all-gather.4.cloned.1.call-done = bf16[128,2,6144]{0,2,1:T(8,128)(2,1)} async-done(((bf16[128,2,768]{0,2,1:T(8,128)(2,1)}), bf16[128,2,6144]{0,2,1:T(8,128)(2,1)}) %all-gather.4.cloned.1.call-update) | async-done | bytes 3145744 | tf_op jit(solution)/shard_map/all_gather | solution.py:30
  74.0 106.3 %all-gather.6.cloned.1.call-done = bf16[12288,3072]{1,0:T(8,128)(2,1)} async-done(((bf16[6144,3072]{1,0:T(8,128)(2,1)}), bf16[12288,3072]{1,0:T(8,128)(2,1)}) %all-gather.6.cloned.1.call-update) | async-done | bytes 75497488 | tf_op jit(solution)/shard_map/all_gather | solution.py:31
  180.2 0.0 copy-done
  180.2 28.6 %fusion.6 = (bf16[128,3072]{1,0:T(8,128)(2,1)}, bf16[128,3072]{1,0:T(8,128)(2,1)}) fusion(bf16[128,3072]{1,0:T(8,128)(2,1)S(1)} %copy-done, bf16[128,12288]{0,1:T(8,128)(2,1)} %bitcast, bf16[12288,3072]{1,0:T(8,128)(2,1)} %all-gather.6.cloned.1.call-done), kind=kOutput, calls=%fused_computation.10 | convolution fusion | flops 9672327168 | bytes 81002496 | tf_op jit(solution)/shard_map/dot_general | solution.py:32
  208.8 0.0 all-gather.8.cloned.1.call-update
  208.8 4.0 all-to-all-start.2
  212.8 7.2 %all-gather.8.cloned.1.call-done = bf16[256,3072]{1,0:T(8,128)(2,1)} async-done(((bf16[128,3072]{1,0:T(8,128)(2,1)}), bf16[256,3072]{1,0:T(8,128)(2,1)}) %all-gather.8.cloned.1.call-update) | async-done | bytes 1572880 | tf_op jit(solution)/shard_map/all_gather | solution.py:42
  219.9 19.3 %fusion.7 = f32[256,6144]{1,0:T(8,128)} fusion(bf16[256,3072]{1,0:T(8,128)(2,1)} %all-gather.8.cloned.1.call-done, bf16[6144,3072]{1,0:T(8,128)(2,1)} %param.4), kind=kOutput, calls=%fused_computation.12 | convolution fusion | flops 9663676416 | bytes 45613056 | tf_op jit(solution)/shard_map/dot_general | solution.py:46
  239.3 6.0 %copy.22 = f32[32,8,8,768]{3,2,0,1:T(8,128)} copy(f32[32,8,8,768]{3,2,1,0:T(8,128)} %bitcast.28) | data formatting | bytes 12582912 | tf_op jit(solution)/shard_map/reshape | solution.py:49
  245.3 0.0 all-to-all-done.2
  245.3 5.8 %all-to-all-start = ((f32[256,8,768]{2,0,1:T(8,128)}), f32[256,8,768]{2,0,1:T(8,128)}, u32[]{:S(2)}, u32[]{:S(2)}) async-start(f32[256,8,768]{2,0,1:T(8,128)} %bitcast.25), calls=%async_computation | async-start | bytes 12582912 | tf_op jit(solution)/shard_map/all_to_all | solution.py:50
  251.1 2.8 copy.17
  253.9 18.0 %convert_bitcast_fusion = bf16[6144,3072]{0,1:T(8,128)(2,1)} fusion(bf16[256,3072]{1,0:T(8,128)(2,1)} %all-gather.8.cloned.1.call-done, bf16[256,6144]{1,0:T(8,128)(2,1)} %bitcast.27), kind=kOutput, calls=%fused_computation | convolution fusion | flops 9682550784 | bytes 42467328 | tf_op jit(solution)/shard_map/dot_general | solution.py:43
  271.9 48.5 %copy.19 = bf16[6144,3072]{1,0:T(8,128)(2,1)} copy(bf16[6144,3072]{0,1:T(8,128)(2,1)} %convert_bitcast_fusion) | data formatting | bytes 75497472
  320.4 69.4 %all-to-all-done = f32[256,8,768]{2,0,1:T(8,128)} async-done(((f32[256,8,768]{2,0,1:T(8,128)}), f32[256,8,768]{2,0,1:T(8,128)}, u32[]{:S(2)}, u32[]{:S(2)}) %all-to-all-start) | async-done | bytes 6291488 | tf_op jit(solution)/shard_map/all_to_all | solution.py:50
  389.8 3.2 reduce_sum.9
  393.0 4.0 %all_to_all.35 = bf16[2,128,1,768]{3,1,2,0:T(8,128)(2,1)S(1)} all-to-all(bf16[2,128,1,768]{3,1,2,0:T(8,128)(2,1)S(1)} %bitcast.30), channel_id=1, replica_groups=mesh['groups'=2,'row'=2,'col'=8] {'row'}, dimensions={0} | all-to-all | bytes 786432 | tf_op jit(solution)/shard_map/all_to_all | solution.py:53
  397.0 1.2 copy.18
Async XLA Ops:
  7.2 66.8 %all-gather.4.cloned.1.call-start = ((), (), s32[]{:S(2)}) async-start(), calls=%async_computation.3 | async-start | bytes 3538944 | tf_op jit(solution)/shard_map/all_gather | solution.py:30
  9.2 171.1 %copy-start = (bf16[128,3072]{1,0:T(8,128)(2,1)S(1)}, bf16[128,3072]{1,0:T(8,128)(2,1)}, u32[]{:S(2)}) copy-start(bf16[128,3072]{1,0:T(8,128)(2,1)} %param.5) | copy-start | bytes 2359300
  9.2 171.0 %all-gather.6.cloned.1.call-start = ((), (), s32[]{:S(2)}) async-start(), calls=%async_computation.4 | async-start | bytes 113246208 | tf_op jit(solution)/shard_map/all_gather | solution.py:31
  9.9 210.0 %all-gather.8.cloned.1.call-start = ((), (), s32[]{:S(2)}) async-start(), calls=%async_computation.5 | async-start | bytes 2359296 | tf_op jit(solution)/shard_map/all_gather | solution.py:42
  208.8 36.5 %all-to-all-start.2 = ((bf16[128,2,6144]{0,2,1:T(8,128)(2,1)}), bf16[128,2,6144]{0,2,1:T(8,128)(2,1)S(1)}, u32[]{:S(2)}, u32[]{:S(2)}) async-start(bf16[128,2,6144]{0,2,1:T(8,128)(2,1)} %all-gather.4.cloned.1.call-done), calls=%async_computation.2 | async-start | bytes 6291456 | tf_op jit(solution)/shard_map/all_to_all | solution.py:37
  245.3 144.5 %all-to-all-start = ((f32[256,8,768]{2,0,1:T(8,128)}), f32[256,8,768]{2,0,1:T(8,128)}, u32[]{:S(2)}, u32[]{:S(2)}) async-start(f32[256,8,768]{2,0,1:T(8,128)} %bitcast.25), calls=%async_computation | async-start | bytes 12582912 | tf_op jit(solution)/shard_map/all_to_all | solution.py:50
Sparse Core Ops, SparseCore 0:
  10.8 63.1 all-gather.3
  75.5 104.6 all-gather.5
  208.9 10.9 all-gather.7
where the time goes:
time: 406 us; the launch traced here: 405 us
  waiting for transfers between devices  248 us (61%)
  matrix products  65.9 us (16%)
  local copies, waits for them, and re-layouts  60.4 us (15%)
  between operations  13.8 us (3%)
  starting transfers between devices  9.85 us (2%)
    all_gather x1, waiting for transfers between devices, local(): weight_cols = lax.all_gather(weights, 'row', axis=0, tiled=True)  106 us
    all_to_all x1, waiting for transfers between devices, local(): lax.all_to_all(split_terms, 'col', split_axis=1, concat_axis=1, tiled=True)  69.4 us
    all_gather x1, waiting for transfers between devices, local(): features = lax.all_gather(inputs, 'col', axis=2, tiled=True)  64 us
    unnamed x5, local copies, waits for them, and re-layouts  51.6 us
    dot_general x1, matrix products, local(): jnp.dot(features.reshape(tok_rows, row_count * half_rows), weight_cols, p...  28.6 us
    dot_general x1, matrix products, local(): lax.dot_general(grad_all, weights, (((1,), (1,)), ((), ())), preferred_el...  19.3 us
    dot_general x1, matrix products, local(): lax.dot_general(own_half, grad_all, (((0,), (0,)), ((), ())), preferred_e...  18 us
  transfers between devices with their start and end apart: 5, of which 4 were waited for; matrix products, arithmetic and copies ran while one was open for 23% of the time, Pallas kernels for 0%

commit v1 on v0

v1 whole, which is shorter than its diff:
```python
import functools
import math

import jax
import jax.numpy as jnp
from jax import lax
from jax.experimental import pallas as pl
from jax.experimental.pallas import tpu as pltpu
from jax.sharding import PartitionSpec as P

root_coef = math.sqrt(2.0 / math.pi)
cube_coef = 0.044715
MESH = pl.DeviceIdType.MESH


def gelu_parts(preact):
    square = preact * preact
    tangent = jnp.tanh(root_coef * (preact + cube_coef * square * preact))
    half = 0.5 * (1.0 + tangent)
    slope = half + 0.5 * preact * (1.0 - tangent * tangent) * root_coef * (
        1.0 + 3.0 * cube_coef * square
    )
    return preact * half, slope


def ring_place(index, count):
    z, x = index // 2, index % 2
    return z * (1 - x) + (count - 1 - z) * x


def ring_column(place, count):
    place = lax.rem(place + 2 * count, count)
    back = place // (count // 2)
    return (1 - back) * (2 * place) + back * (2 * (count - 1 - place) + 1)


def exchange_kernel(
    count, tile, split,
    x_ref, w_ref, ga_ref,
    act_ref, own_ref, gradall_ref, sum_ref, term_ref,
    feats, wv, acc, xbuf, grad, term, outgo, income,
    w_sem, swap_sem, ring_send, ring_recv, part_sem, gp_sem, rs_send, rs_recv, out_sem,
):
    half = count // 2
    tok = x_ref.shape[1]
    piece = x_ref.shape[2]
    hidden = w_ref.shape[1]
    tiles = hidden // tile
    r = lax.axis_index("row")
    c = lax.axis_index("col")
    p = ring_place(c, count)
    near = (ring_column(p + 1, count), ring_column(p - 1, count))
    other = {"row": 1 - r}

    order = [0]
    for s in range(1, half + 1):
        order += [-s] if s == half else [-s, s]
    columns = {o: ring_column(p + o, count) for o in order}
    columns[half] = columns[-half]

    def rows_of(q):
        h = lax.rem(r + q, 2)
        return pl.ds(pl.multiple_of(h * tok, tok), tok)

    w_copies = {}
    for j, o in enumerate(order):
        k = columns[o]
        w_copies[o] = pltpu.make_async_copy(
            w_ref.at[pl.ds(pl.multiple_of(k * piece, piece), piece)], wv.at[k], w_sem.at[j]
        )
        w_copies[o].start()

    barrier = pltpu.get_barrier_semaphore()
    for target in ({"col": near[0]}, {"col": near[1]}, other):
        pl.semaphore_signal(barrier, inc=1, device_id=target, device_id_type=MESH)
    pl.semaphore_wait(barrier, 3)

    def ring_copy(d, s, q):
        o = -(s - 1) if d == 0 else s - 1
        k = columns[o]
        part = feats.at[k, rows_of(q)]
        return pltpu.make_async_remote_copy(
            src_ref=part, dst_ref=part,
            send_sem=ring_send.at[d, s - 1, q], recv_sem=ring_recv.at[d, s - 1, q],
            device_id={"col": near[d]}, device_id_type=MESH,
        )

    def ring_arrival(d, s, q):
        o = -s if d == 0 else s
        part = feats.at[columns[o], rows_of(q)]
        return pltpu.make_async_remote_copy(
            src_ref=part, dst_ref=part,
            send_sem=ring_send.at[d, s - 1, q], recv_sem=ring_recv.at[d, s - 1, q],
            device_id={"col": near[d]}, device_id_type=MESH,
        )

    def used(d, s, q):
        return s < half or (s == half and q == d)

    swap = pltpu.make_async_remote_copy(
        src_ref=x_ref.at[1 - r], dst_ref=feats.at[c, rows_of(0)],
        send_sem=swap_sem.at[0], recv_sem=swap_sem.at[1],
        device_id=other, device_id_type=MESH,
    )
    swap.start()
    feats[c, rows_of(0), :] = x_ref[r]
    sent = []
    for d in range(2):
        if used(d, 1, 0):
            copy = ring_copy(d, 1, 0)
            copy.start()
            sent.append(copy)
    arrived = pltpu.make_async_remote_copy(
        src_ref=x_ref.at[1 - r], dst_ref=feats.at[c, rows_of(1)],
        send_sem=swap_sem.at[0], recv_sem=swap_sem.at[1],
        device_id=other, device_id_type=MESH,
    )
    arrived.wait_recv()
    for d in range(2):
        if used(d, 1, 1):
            copy = ring_copy(d, 1, 1)
            copy.start()
            sent.append(copy)

    def project(o):
        k = columns[o]
        w_copies[o].wait()

        @pl.loop(0, tiles)
        def _(t):
            cols = pl.ds(pl.multiple_of(t * tile, tile), tile)
            product = jnp.dot(feats[k], wv[k, :, cols], preferred_element_type=jnp.float32)
            if o == 0:
                acc[t] = product
            else:
                acc[t] = acc[t] + product
            if o == order[-1]:
                part_copy(t).start()

    def part_copy(t):
        return pltpu.make_async_remote_copy(
            src_ref=acc.at[t, rows_of(1)], dst_ref=xbuf.at[t],
            send_sem=part_sem.at[0, t], recv_sem=part_sem.at[1, t],
            device_id=other, device_id_type=MESH,
        )

    pending = [0]
    for s in range(1, half + 1):
        for q in range(2):
            for d in range(2):
                if used(d, s, q):
                    ring_arrival(d, s, q).wait_recv()
                    if used(d, s + 1, q):
                        copy = ring_copy(d, s + 1, q)
                        copy.start()
                        sent.append(copy)
            if pending:
                project(pending.pop(0))
        for o in pending:
            project(o)
        pending = [-s] if s == half else [-s, s]
    for o in pending:
        project(o)

    own_copies = []
    for j, o in enumerate(order):
        k = columns[o]
        copy = pltpu.make_async_copy(
            feats.at[k], own_ref.at[:, pl.ds(pl.multiple_of(k * piece, piece), piece)], out_sem.at[j]
        )
        copy.start()
        own_copies.append(copy)

    mine, theirs = rows_of(0), rows_of(1)

    def grad_copy(t):
        part = grad.at[mine, pl.ds(pl.multiple_of(t * tile, tile), tile)]
        return pltpu.make_async_remote_copy(
            src_ref=part, dst_ref=part,
            send_sem=gp_sem.at[0, t], recv_sem=gp_sem.at[1, t],
            device_id=other, device_id_type=MESH,
        )

    @pl.loop(0, tiles)
    def _(t):
        cols = pl.ds(pl.multiple_of(t * tile, tile), tile)
        part_copy(t).wait_recv()
        value, slope = gelu_parts(acc[t, mine, :] + xbuf[t])
        act_ref[:, cols] = value.astype(act_ref.dtype)
        grad[mine, cols] = (ga_ref[:, cols].astype(jnp.float32) * slope).astype(grad.dtype)
        grad_copy(t).start()

    @pl.loop(0, tiles)
    def _(t):
        cols = pl.ds(pl.multiple_of(t * tile, tile), tile)
        part = grad.at[theirs, cols]
        pltpu.make_async_remote_copy(
            src_ref=part, dst_ref=part,
            send_sem=gp_sem.at[0, t], recv_sem=gp_sem.at[1, t],
            device_id=other, device_id_type=MESH,
        ).wait_recv()

    gradall_copy = pltpu.make_async_copy(grad, gradall_ref, out_sem.at[count])
    gradall_copy.start()

    def back_project(o, into):
        k = columns[o]

        @pl.loop(0, piece // split)
        def _(j):
            part = pl.ds(pl.multiple_of(j * split, split), split)
            into[:, part] = lax.dot_general(
                grad[...], wv[k, part, :], (((1,), (1,)), ((), ())),
                preferred_element_type=jnp.float32,
            )

    def sum_copy(d, s, q):
        return pltpu.make_async_remote_copy(
            src_ref=outgo.at[d, s - 1, rows_of(q)], dst_ref=income.at[d, s - 1, rows_of(q)],
            send_sem=rs_send.at[d, s - 1, q], recv_sem=rs_recv.at[d, s - 1, q],
            device_id={"col": near[d]}, device_id_type=MESH,
        )

    def sum_used(d, s, q):
        return s > 1 or q == d

    for s in range(1, half + 1):
        far = half - s + 1
        if s == 1:
            back_project(-far, term.at[0])
        else:
            back_project(far, term.at[0])
            back_project(-far, term.at[1])
        for late in (False, True):
            for q in range(2):
                for d in range(2):
                    if not sum_used(d, s, q):
                        continue
                    has_sum = s > 1 and sum_used(d, s - 1, q)
                    if has_sum != late:
                        continue
                    rows = rows_of(q)
                    value = term[0 if s == 1 else d, rows, :]
                    if has_sum:
                        sum_copy(d, s - 1, q).wait_recv()
                        value = value + income[d, s - 2, rows, :].astype(jnp.float32)
                    if s < half:
                        outgo[d, s - 1, rows, :] = value.astype(outgo.dtype)
                        copy = sum_copy(d, s, q)
                        copy.start()
                        sent.append(copy)
                    else:
                        sum_ref[d, rows, :] = value.astype(sum_ref.dtype)
    back_project(0, term_ref)

    swap.wait_send()
    for copy in sent:
        copy.wait_send()
    for copy in own_copies:
        copy.wait()
    gradall_copy.wait()

    @pl.loop(0, tiles)
    def _(t):
        part_copy(t).wait_send()
        grad_copy(t).wait_send()


def exchange(x_halves, weights, grad_act, count):
    _, tok, piece = x_halves.shape
    half_rows, hidden = weights.shape
    half = count // 2
    tile = 512 if hidden % 512 == 0 else 128
    split = 256 if piece % 256 == 0 else 128
    tiles = hidden // tile
    all_tok = 2 * tok
    vmem = pl.BlockSpec(memory_space=pltpu.VMEM)
    hbm = pl.BlockSpec(memory_space=pl.ANY)
    bf16, f32 = jnp.bfloat16, jnp.float32
    dma = pltpu.SemaphoreType.DMA
    return pl.pallas_call(
        functools.partial(exchange_kernel, count, tile, split),
        out_shape=(
            jax.ShapeDtypeStruct((tok, hidden), bf16),
            jax.ShapeDtypeStruct((all_tok, half_rows), bf16),
            jax.ShapeDtypeStruct((all_tok, hidden), bf16),
            jax.ShapeDtypeStruct((2, all_tok, piece), bf16),
            jax.ShapeDtypeStruct((all_tok, piece), f32),
        ),
        in_specs=[vmem, hbm, vmem],
        out_specs=(vmem, hbm, hbm, vmem, vmem),
        scratch_shapes=[
            pltpu.VMEM((count, all_tok, piece), bf16),
            pltpu.VMEM((count, piece, hidden), bf16),
            pltpu.VMEM((tiles, all_tok, tile), f32),
            pltpu.VMEM((tiles, tok, tile), f32),
            pltpu.VMEM((all_tok, hidden), bf16),
            pltpu.VMEM((2, all_tok, piece), f32),
            pltpu.VMEM((2, half - 1, all_tok, piece), bf16),
            pltpu.VMEM((2, half - 1, all_tok, piece), bf16),
            dma((count,)),
            dma((2,)),
            dma((2, half, 2)),
            dma((2, half, 2)),
            dma((2, tiles)),
            dma((2, tiles)),
            dma((2, half - 1, 2)),
            dma((2, half - 1, 2)),
            dma((count + 1,)),
        ],
        compiler_params=pltpu.CompilerParams(
            collective_id=0, has_side_effects=True, vmem_limit_bytes=62 * 1024 * 1024
        ),
        cost_estimate=pl.CostEstimate(
            flops=4 * all_tok * half_rows * hidden,
            bytes_accessed=2 * half_rows * hidden,
            transcendentals=tok * hidden,
        ),
    )(x_halves, weights, grad_act)


def weight_gradient(own_half, grad_all):
    return lax.dot_general(
        own_half, grad_all, (((0,), (0,)), ((), ())), preferred_element_type=jnp.float32
    ).astype(jnp.bfloat16)


def local(inputs, weights, grad_act):
    tok_rows, row_count, piece_cols = inputs.shape
    all_tokens = tok_rows * row_count
    col_count = lax.axis_size("col")
    x_halves = jnp.transpose(inputs, (1, 0, 2))
    activation, own_half, grad_all, sums, own_term = exchange(x_halves, weights, grad_act, col_count)
    ring = [ring_column_static(place, col_count) for place in range(col_count)]
    onward = [(ring[i], ring[(i + 1) % col_count]) for i in range(col_count)]
    backward = [(target, source) for source, target in onward]
    from_left = lax.ppermute(sums[0], "col", onward)
    from_right = lax.ppermute(sums[1], "col", backward)
    grad_w = weight_gradient(own_half, grad_all)
    summed = own_term + from_left.astype(jnp.float32) + from_right.astype(jnp.float32)
    arranged = summed.astype(jnp.bfloat16).reshape(row_count, tok_rows, 1, piece_cols)
    moved = lax.all_to_all(arranged, "row", split_axis=0, concat_axis=2, tiled=True)
    return (activation, moved.reshape(tok_rows, row_count, piece_cols), grad_w)


def ring_column_static(place, count):
    return 2 * place if place < count // 2 else 2 * (count - 1 - place) + 1


def plain(inputs, weights, grad_act):
    tok_rows, row_count, piece_cols = inputs.shape
    half_rows, hid_cols = weights.shape
    all_tokens = tok_rows * row_count
    col_count = lax.axis_size("col")
    own = lax.all_to_all(inputs, "row", split_axis=1, concat_axis=0, tiled=True)
    own_half = lax.all_gather(own.reshape(all_tokens, piece_cols), "col", axis=1, tiled=True)
    partial = jnp.dot(own_half, weights, preferred_element_type=jnp.float32)
    preact = lax.psum_scatter(partial, "row", scatter_dimension=0, tiled=True)
    value, slope = gelu_parts(preact)
    activation = value.astype(jnp.bfloat16)
    grad_pre = (grad_act.astype(jnp.float32) * slope).astype(jnp.bfloat16)
    grad_all = lax.all_gather(grad_pre, "row", axis=0, tiled=True)
    grad_w = weight_gradient(own_half, grad_all)
    local_terms = lax.dot_general(
        grad_all, weights, (((1,), (1,)), ((), ())), preferred_element_type=jnp.float32
    )
    split_terms = local_terms.reshape(all_tokens, col_count, piece_cols)
    received = lax.all_to_all(split_terms, "col", split_axis=1, concat_axis=1, tiled=True)
    summed = jnp.sum(received, axis=1).astype(jnp.bfloat16)
    arranged = summed.reshape(row_count, tok_rows, 1, piece_cols)
    moved = lax.all_to_all(arranged, "row", split_axis=0, concat_axis=2, tiled=True)
    return (activation, moved.reshape(tok_rows, row_count, piece_cols), grad_w)


def solution(mesh):
    placed = (P(("groups", "row"), None, "col"), P("row", "col"), P(("groups", "row"), "col"))

    def by_shape(inputs, weights, grad_act):
        tok_rows, row_count, piece_cols = inputs.shape
        hid_cols = weights.shape[1]
        fits = (
            row_count == 2
            and mesh.shape["col"] in (4, 6, 8)
            and tok_rows % 16 == 0
            and piece_cols % 128 == 0
            and hid_cols % 128 == 0
        )
        return (local if fits else plain)(inputs, weights, grad_act)

    return jax.shard_map(
        by_shape,
        mesh=mesh,
        in_specs=placed,
        out_specs=(
            P(("groups", "row"), "col"),
            P(("groups", "row"), None, "col"),
            P(("groups", "row"), "col"),
        ),
        check_vma=False,
    )
```

time: 406 us -> 107 us (0.26)
  waiting for transfers between devices: 248 us -> 0.01 us
  Pallas kernels: 0 us -> 76.9 us
  local copies, waits for them, and re-layouts: 60.4 us -> 4.99 us
  matrix products: 65.9 us -> 18.3 us
  between operations: 13.8 us -> 0.66 us
  starting transfers between devices: 9.85 us -> 2.08 us
    all_gather x3 -> x0, waiting for transfers between devices: 177 us -> none  [the longest x1 106 us: local(): weight_cols = lax.all_gather(weights, 'row', axis=0, tiled=True)]
    pallas_call x0 -> x1, Pallas kernels: none -> 76.9 us  [exchange(): pl.pallas_call(functools.partial(exchange_kernel, count, tile, split), ou...]
    all_to_all x2 -> x0, waiting for transfers between devices: 69.4 us -> none  [the longest x1 69.4 us: local(): lax.all_to_all(split_terms, 'col', split_axis=1, concat_axis=1, tiled=True)]
    unnamed x5 -> x7, local copies, waits for them, and re-layouts: 51.6 us -> 3.82 us
    dot_general x3 -> x1, matrix products: 65.9 us -> 18.3 us  [weight_gradient(): lax.dot_general(own_half, grad_all, (((0,), (0,)), ((), ())), preferred_e...]
    all_to_all x2 -> x0, starting transfers between devices: 9.73 us -> none  [the longest x1 5.78 us: local(): lax.all_to_all(split_terms, 'col', split_axis=1, concat_axis=1, tiled=True)]
    reshape x1 -> x0, local copies, waits for them, and re-layouts: 6.03 us -> none  [local(): split_terms = local_terms.reshape(all_tokens, col_count, piece_cols)]
  transfers between devices with their start and end apart: 5 -> 2, of which waited for: 4 -> 0; matrix products, arithmetic and copies ran while one was open for 23% -> 17% of each run, Pallas kernels for 0% -> 0%
where the time goes in v1:
time: 107 us
  Pallas kernels  76.9 us (72%)
  matrix products  18.3 us (17%)
  local copies, waits for them, and re-layouts  4.99 us (5%)
  blocking collectives  4.18 us (4%)
  starting transfers between devices  2.08 us (2%)
    pallas_call x1, Pallas kernels, exchange(): pl.pallas_call(functools.partial(exchange_kernel, count, tile, split), ou...  76.9 us
    dot_general x1, matrix products, weight_gradient(): lax.dot_general(own_half, grad_all, (((0,), (0,)), ((), ())), preferred_e...  18.3 us
    all_to_all x1, blocking collectives, local(): lax.all_to_all(arranged, 'row', split_axis=0, concat_axis=2, tiled=True)  4.18 us
    unnamed x7, local copies, waits for them, and re-layouts  3.82 us
  transfers between devices with their start and end apart: 2, of which 0 were waited for; matrix products, arithmetic and copies ran while one was open for 17% of the time, Pallas kernels for 0%

profile of v1, /device:TPU:0, one launch (start us, length us, event | category | flops | bytes accessed | tf_op | source)
XLA Modules:
  0.0 107.2 jit_solution(12761028915755041969)
XLA Ops:
  0.6 1.8 %copy.12 = bf16[128,2,768]{2,0,1:T(8,128)(2,1)} copy(bf16[128,2,768]{2,1,0:T(2,128)(2,1)} %param.3) | data formatting | bytes 786432 | tf_op args[0]
  2.4 76.9 %shard_map.58 = (bf16[128,3072]{1,0:T(8,128)(2,1)}, bf16[256,6144]{1,0:T(8,128)(2,1)}, bf16[256,3072]{1,0:T(8,128)(2,1)}, bf16[2,256,768]{2,1,0:T(8,128)(2,1)}, f32[256,768]{1,0:T(8,128)}) custom-call(bf16[2,128,768]{2,1,0:T(8,128)(2,1)} %bitcast.19, bf16[6144,3072]{1,0:T(8,128)(2,1)} %w_ref.1, bf16[128,3072]{1,0:T(8,128)(2,1)} %ga_ref.1), custom_call_target="tpu_custom_call" | custom-call | flops 19327352832 | bytes 37748736 | tf_op jit(solution)/shard_map/pallas_call | solution.py:281
  79.3 1.2 %slice_bitcast_fusion.1 = (bf16[256,768]{1,0:T(8,128)(2,1)S(1)}, bf16[256,768]{1,0:T(8,128)(2,1)S(1)}) fusion(bf16[2,256,768]{2,1,0:T(8,128)(2,1)} %get-tuple-element.10), kind=kLoop, calls=%fused_computation.4 | loop fusion | bytes 1572864 | tf_op jit(solution)/shard_map/squeeze | solution.py:337
  80.5 0.5 collective-permute-start
  81.0 1.6 %collective-permute-start.1 = (bf16[256,768]{1,0:T(8,128)(2,1)S(1)}, bf16[256,768]{1,0:T(8,128)(2,1)S(1)}, u32[]{:S(2)}, u32[]{:S(2)}) collective-permute-start(bf16[256,768]{1,0:T(8,128)(2,1)S(1)} %get-tuple-element.17), channel_id=1, source_target_pairs={{2,0},{4,2},{6,4},{7,6},{5,7},{3,5},{1,3},{0,1},{10,8},{12,10},{14... | collective-permute-start | bytes 1179656 | tf_op jit(solution)/shard_map/ppermute | solution.py:338
  82.5 0.0 copy-start.1
  82.5 18.3 %convolution_convert_fusion = bf16[6144,3072]{1,0:T(8,128)(2,1)} fusion(bf16[256,6144]{1,0:T(8,128)(2,1)} %get-tuple-element.11, bf16[256,3072]{1,0:T(8,128)(2,1)} %get-tuple-element.12), kind=kOutput, calls=%fused_computation | convolution fusion | flops 9682550784 | bytes 42467328 | tf_op jit(solution)/shard_map/dot_general | solution.py:323
  100.8 0.0 copy-start
  100.8 0.0 collective-permute-done
  100.8 0.0 collective-permute-done.1
  100.8 0.0 copy-done.1
  100.9 0.1 add_convert_fusion
  101.0 4.2 %all_to_all.15 = bf16[2,128,1,768]{3,1,2,0:T(8,128)(2,1)S(1)} all-to-all(bf16[2,128,1,768]{3,1,2,0:T(8,128)(2,1)S(1)} %bitcast.18), channel_id=1, replica_groups=mesh['groups'=2,'row'=2,'col'=8] {'row'}, dimensions={0} | all-to-all | bytes 786432 | tf_op jit(solution)/shard_map/all_to_all | solution.py:342
  105.2 1.2 %copy.10 = bf16[128,2,768]{2,1,0:T(2,128)(2,1)} copy(bf16[128,2,768]{2,0,1:T(8,128)(2,1)S(1)} %bitcast.17) | data formatting | bytes 786432
  106.3 0.0 copy-done
  106.3 0.9 copy.14
Async XLA Ops:
  80.5 20.4 %collective-permute-start = (bf16[256,768]{1,0:T(8,128)(2,1)S(1)}, bf16[256,768]{1,0:T(8,128)(2,1)S(1)}, u32[]{:S(2)}, u32[]{:S(2)}) collective-permute-start(bf16[256,768]{1,0:T(8,128)(2,1)S(1)} %get-tuple-element.16), channel_id=1, source_target_pairs={{0,2},{2,4},{4,6},{6,7},{7,5},{5,3},{3,1},{1,0},{8,10},{10,12},{12... | collective-permute-start | bytes 1179656 | tf_op jit(solution)/shard_map/ppermute | solution.py:337
  81.0 19.9 %collective-permute-start.1 = (bf16[256,768]{1,0:T(8,128)(2,1)S(1)}, bf16[256,768]{1,0:T(8,128)(2,1)S(1)}, u32[]{:S(2)}, u32[]{:S(2)}) collective-permute-start(bf16[256,768]{1,0:T(8,128)(2,1)S(1)} %get-tuple-element.17), channel_id=1, source_target_pairs={{2,0},{4,2},{6,4},{7,6},{5,7},{3,5},{1,3},{0,1},{10,8},{12,10},{14... | collective-permute-start | bytes 1179656 | tf_op jit(solution)/shard_map/ppermute | solution.py:338
  82.5 18.3 %copy-start.1 = (f32[256,768]{1,0:T(8,128)S(1)}, f32[256,768]{1,0:T(8,128)}, u32[]{:S(2)}) copy-start(f32[256,768]{1,0:T(8,128)} %get-tuple-element.9) | copy-start | bytes 2359300
  100.8 5.5 %copy-start = (bf16[128,3072]{1,0:T(8,128)(2,1)S(1)}, bf16[128,3072]{1,0:T(8,128)(2,1)}, u32[]{:S(2)}) copy-start(bf16[128,3072]{1,0:T(8,128)(2,1)} %get-tuple-element.21) | copy-start | bytes 2359300

commit v2 on v1

--- a/solution.py
+++ b/solution.py
@@ -37,7 +37,7 @@
 def exchange_kernel(
     count, tile, split,
     x_ref, w_ref, ga_ref,
-    act_ref, own_ref, gradall_ref, sum_ref, term_ref,
+    act_ref, own_ref, gradall_ref, sum_right, sum_left, term_right, term_left, term_mine, term_theirs,
     feats, wv, acc, xbuf, grad, term, outgo, income,
     w_sem, swap_sem, ring_send, ring_recv, part_sem, gp_sem, rs_send, rs_recv, out_sem,
 ):
@@ -59,8 +59,7 @@
     columns[half] = columns[-half]
 
     def rows_of(q):
-        h = lax.rem(r + q, 2)
-        return pl.ds(pl.multiple_of(h * tok, tok), tok)
+        return pl.ds(q * tok, tok)
 
     w_copies = {}
     for j, o in enumerate(order):
@@ -98,7 +97,7 @@
         return s < half or (s == half and q == d)
 
     swap = pltpu.make_async_remote_copy(
-        src_ref=x_ref.at[1 - r], dst_ref=feats.at[c, rows_of(0)],
+        src_ref=x_ref.at[1 - r], dst_ref=feats.at[c, rows_of(1)],
         send_sem=swap_sem.at[0], recv_sem=swap_sem.at[1],
         device_id=other, device_id_type=MESH,
     )
@@ -110,12 +109,7 @@
             copy = ring_copy(d, 1, 0)
             copy.start()
             sent.append(copy)
-    arrived = pltpu.make_async_remote_copy(
-        src_ref=x_ref.at[1 - r], dst_ref=feats.at[c, rows_of(1)],
-        send_sem=swap_sem.at[0], recv_sem=swap_sem.at[1],
-        device_id=other, device_id_type=MESH,
-    )
-    arrived.wait_recv()
+    swap.wait_recv()
     for d in range(2):
         if used(d, 1, 1):
             copy = ring_copy(d, 1, 1)
@@ -174,9 +168,9 @@
     mine, theirs = rows_of(0), rows_of(1)
 
     def grad_copy(t):
-        part = grad.at[mine, pl.ds(pl.multiple_of(t * tile, tile), tile)]
+        cols = pl.ds(pl.multiple_of(t * tile, tile), tile)
         return pltpu.make_async_remote_copy(
-            src_ref=part, dst_ref=part,
+            src_ref=grad.at[mine, cols], dst_ref=grad.at[theirs, cols],
             send_sem=gp_sem.at[0, t], recv_sem=gp_sem.at[1, t],
             device_id=other, device_id_type=MESH,
         )
@@ -192,13 +186,7 @@
 
     @pl.loop(0, tiles)
     def _(t):
-        cols = pl.ds(pl.multiple_of(t * tile, tile), tile)
-        part = grad.at[theirs, cols]
-        pltpu.make_async_remote_copy(
-            src_ref=part, dst_ref=part,
-            send_sem=gp_sem.at[0, t], recv_sem=gp_sem.at[1, t],
-            device_id=other, device_id_type=MESH,
-        ).wait_recv()
+        grad_copy(t).wait_recv()
 
     gradall_copy = pltpu.make_async_copy(grad, gradall_ref, out_sem.at[count])
     gradall_copy.start()
@@ -209,14 +197,22 @@
         @pl.loop(0, piece // split)
         def _(j):
             part = pl.ds(pl.multiple_of(j * split, split), split)
-            into[:, part] = lax.dot_general(
-                grad[...], wv[k, part, :], (((1,), (1,)), ((), ())),
+            value = lax.dot_general(
+                wv[k, part, :], grad[...], (((1,), (1,)), ((), ())),
                 preferred_element_type=jnp.float32,
             )
+            if len(into) == 1:
+                into[0][part, :] = value
+            else:
+                into[0][part, :] = value[:, :tok]
+                into[1][part, :] = value[:, tok:]
+
+    def feature_rows(q):
+        return pl.ds(q * (piece // 2), piece // 2)
 
     def sum_copy(d, s, q):
         return pltpu.make_async_remote_copy(
-            src_ref=outgo.at[d, s - 1, rows_of(q)], dst_ref=income.at[d, s - 1, rows_of(q)],
+            src_ref=outgo.at[d, s - 1, feature_rows(q)], dst_ref=income.at[d, s - 1, feature_rows(q)],
             send_sem=rs_send.at[d, s - 1, q], recv_sem=rs_recv.at[d, s - 1, q],
             device_id={"col": near[d]}, device_id_type=MESH,
         )
@@ -224,13 +220,16 @@
     def sum_used(d, s, q):
         return s > 1 or q == d
 
-    for s in range(1, half + 1):
+    for s in range(1, half):
         far = half - s + 1
         if s == 1:
-            back_project(-far, term.at[0])
+            back_project(-far, [term.at[0]])
         else:
-            back_project(far, term.at[0])
-            back_project(-far, term.at[1])
+            back_project(far, [term.at[0]])
+            back_project(-far, [term.at[1]])
+        if s == half - 1:
+            back_project(1, [term_right])
+            back_project(-1, [term_left])
         for late in (False, True):
             for q in range(2):
                 for d in range(2):
@@ -239,19 +238,20 @@
                     has_sum = s > 1 and sum_used(d, s - 1, q)
                     if has_sum != late:
                         continue
-                    rows = rows_of(q)
+                    rows = feature_rows(q)
                     value = term[0 if s == 1 else d, rows, :]
                     if has_sum:
                         sum_copy(d, s - 1, q).wait_recv()
                         value = value + income[d, s - 2, rows, :].astype(jnp.float32)
-                    if s < half:
+                    if s < half - 1:
                         outgo[d, s - 1, rows, :] = value.astype(outgo.dtype)
                         copy = sum_copy(d, s, q)
                         copy.start()
                         sent.append(copy)
                     else:
-                        sum_ref[d, rows, :] = value.astype(sum_ref.dtype)
-    back_project(0, term_ref)
+                        (sum_right, sum_left)[d][rows, :] = value.astype(sum_right.dtype)
+        if s == half - 2:
+            back_project(0, [term_mine, term_theirs])
 
     swap.wait_send()
     for copy in sent:
@@ -271,7 +271,7 @@
     half_rows, hidden = weights.shape
     half = count // 2
     tile = 512 if hidden % 512 == 0 else 128
-    split = 256 if piece % 256 == 0 else 128
+    split = piece
     tiles = hidden // tile
     all_tok = 2 * tok
     vmem = pl.BlockSpec(memory_space=pltpu.VMEM)
@@ -284,28 +284,32 @@
             jax.ShapeDtypeStruct((tok, hidden), bf16),
             jax.ShapeDtypeStruct((all_tok, half_rows), bf16),
             jax.ShapeDtypeStruct((all_tok, hidden), bf16),
-            jax.ShapeDtypeStruct((2, all_tok, piece), bf16),
-            jax.ShapeDtypeStruct((all_tok, piece), f32),
+            jax.ShapeDtypeStruct((piece, all_tok), bf16),
+            jax.ShapeDtypeStruct((piece, all_tok), bf16),
+            jax.ShapeDtypeStruct((piece, all_tok), f32),
+            jax.ShapeDtypeStruct((piece, all_tok), f32),
+            jax.ShapeDtypeStruct((piece, tok), f32),
+            jax.ShapeDtypeStruct((piece, tok), f32),
         ),
         in_specs=[vmem, hbm, vmem],
-        out_specs=(vmem, hbm, hbm, vmem, vmem),
+        out_specs=(vmem, hbm, hbm) + (vmem,) * 6,
         scratch_shapes=[
             pltpu.VMEM((count, all_tok, piece), bf16),
             pltpu.VMEM((count, piece, hidden), bf16),
             pltpu.VMEM((tiles, all_tok, tile), f32),
             pltpu.VMEM((tiles, tok, tile), f32),
             pltpu.VMEM((all_tok, hidden), bf16),
-            pltpu.VMEM((2, all_tok, piece), f32),
-            pltpu.VMEM((2, half - 1, all_tok, piece), bf16),
-            pltpu.VMEM((2, half - 1, all_tok, piece), bf16),
+            pltpu.VMEM((2, piece, all_tok), f32),
+            pltpu.VMEM((2, half - 2, piece, all_tok), bf16),
+            pltpu.VMEM((2, half - 2, piece, all_tok), bf16),
             dma((count,)),
             dma((2,)),
             dma((2, half, 2)),
             dma((2, half, 2)),
             dma((2, tiles)),
             dma((2, tiles)),
-            dma((2, half - 1, 2)),
-            dma((2, half - 1, 2)),
+            dma((2, half - 2, 2)),
+            dma((2, half - 2, 2)),
             dma((count + 1,)),
         ],
         compiler_params=pltpu.CompilerParams(
@@ -325,22 +329,79 @@
     ).astype(jnp.bfloat16)
 
 
+def gradient_kernel(own_ref, grad_ref, *rest):
+    out_ref = rest[-1]
+    out_ref[...] = lax.dot_general(
+        own_ref[...], grad_ref[...], (((0,), (0,)), ((), ())), preferred_element_type=jnp.float32
+    ).astype(out_ref.dtype)
+
+
+def gradient_rows(own_half, grad_all, block, first, blocks, filled=None):
+    tokens, features = own_half.shape
+    hidden = grad_all.shape[1]
+    in_specs = [
+        pl.BlockSpec((tokens, block), lambda i: (0, i + first)),
+        pl.BlockSpec((tokens, hidden), lambda i: (0, 0)),
+    ]
+    operands = [own_half, grad_all]
+    if filled is not None:
+        in_specs.append(pl.BlockSpec(memory_space=pl.ANY))
+        operands.append(filled)
+    return pl.pallas_call(
+        gradient_kernel,
+        grid=(blocks,),
+        out_shape=jax.ShapeDtypeStruct((features, hidden), jnp.bfloat16),
+        in_specs=in_specs,
+        out_specs=pl.BlockSpec((block, hidden), lambda i: (i + first, 0)),
+        input_output_aliases={} if filled is None else {2: 0},
+        compiler_params=pltpu.CompilerParams(vmem_limit_bytes=60 * 1024 * 1024),
+        cost_estimate=pl.CostEstimate(
+            flops=2 * tokens * block * blocks * hidden,
+            bytes_accessed=2 * (block * blocks * (hidden + tokens) + tokens * hidden),
+            transcendentals=0,
+        ),
+    )(*operands)
+
+
 def local(inputs, weights, grad_act):
-    tok_rows, row_count, piece_cols = inputs.shape
-    all_tokens = tok_rows * row_count
-    col_count = lax.axis_size("col")
+    tok, _, piece = inputs.shape
+    half_rows = weights.shape[0]
+    count = lax.axis_size("col")
+    f32, bf16 = jnp.float32, jnp.bfloat16
     x_halves = jnp.transpose(inputs, (1, 0, 2))
-    activation, own_half, grad_all, sums, own_term = exchange(x_halves, weights, grad_act, col_count)
-    ring = [ring_column_static(place, col_count) for place in range(col_count)]
-    onward = [(ring[i], ring[(i + 1) % col_count]) for i in range(col_count)]
+    (
+        activation, own_half, grad_all,
+        sum_right, sum_left, term_right, term_left, term_mine, term_theirs,
+    ) = exchange(x_halves, weights, grad_act, count)
+    ring = [ring_column_static(place, count) for place in range(count)]
+    onward = [(ring[i], ring[(i + 1) % count]) for i in range(count)]
     backward = [(target, source) for source, target in onward]
-    from_left = lax.ppermute(sums[0], "col", onward)
-    from_right = lax.ppermute(sums[1], "col", backward)
-    grad_w = weight_gradient(own_half, grad_all)
-    summed = own_term + from_left.astype(jnp.float32) + from_right.astype(jnp.float32)
-    arranged = summed.astype(jnp.bfloat16).reshape(row_count, tok_rows, 1, piece_cols)
-    moved = lax.all_to_all(arranged, "row", split_axis=0, concat_axis=2, tiled=True)
-    return (activation, moved.reshape(tok_rows, row_count, piece_cols), grad_w)
+    crossed = [
+        [(row * count + a, (1 - row) * count + b) for row in range(2) for a, b in hops]
+        for hops in (onward, backward)
+    ]
+    from_left = lax.ppermute(sum_right, "col", onward)
+    from_right = lax.ppermute(sum_left, "col", backward)
+    theirs_own = lax.ppermute(term_theirs, "row", [(0, 1), (1, 0)])
+    first = count // 2
+    grad_w = gradient_rows(own_half, grad_all, piece, 0, first)
+    to_right = (term_right + from_left.astype(f32)).astype(bf16)
+    to_left = (term_left + from_right.astype(f32)).astype(bf16)
+    mine = [
+        lax.ppermute(to_right[:, :tok], "col", onward),
+        lax.ppermute(to_left[:, :tok], "col", backward),
+    ]
+    theirs = [
+        lax.ppermute(to_right[:, tok:], ("row", "col"), crossed[0]),
+        lax.ppermute(to_left[:, tok:], ("row", "col"), crossed[1]),
+    ]
+    grad_w = gradient_rows(own_half, grad_all, piece, first, count - first, grad_w)
+    mine = (term_mine + mine[0].astype(f32) + mine[1].astype(f32)).astype(bf16)
+    theirs = (theirs_own + theirs[0].astype(f32) + theirs[1].astype(f32)).astype(bf16)
+    upper = lax.axis_index("row") == 0
+    halves = jnp.stack([jnp.where(upper, mine, theirs), jnp.where(upper, theirs, mine)])
+    grad_x = jnp.transpose(halves, (2, 0, 1))
+    return (activation, grad_x, grad_w)
 
 
 def ring_column_static(place, count):
@@ -380,7 +441,7 @@
         hid_cols = weights.shape[1]
         fits = (
             row_count == 2
-            and mesh.shape["col"] in (4, 6, 8)
+            and mesh.shape["col"] in (6, 8, 10)
             and tok_rows % 16 == 0
             and piece_cols % 128 == 0
             and hid_cols % 128 == 0

time: 107 us -> 97.2 us (0.908)
  matrix products: 18.3 us -> 0 us
  Pallas kernels: 76.9 us -> 86.3 us
  blocking collectives: 4.18 us -> 0 us
  starting transfers between devices: 2.08 us -> 5.68 us
  local copies, waits for them, and re-layouts: 4.99 us -> 3.8 us
    pallas_call x0 -> x2, Pallas kernels: none -> 20.6 us  [gradient_rows(): pl.pallas_call(gradient_kernel, grid=(blocks,), out_shape=jax.ShapeDtypeS...]
    dot_general x1 -> x0, matrix products: 18.3 us -> none  [weight_gradient(): lax.dot_general(own_half, grad_all, (((0,), (0,)), ((), ())), preferred_e...]
    pallas_call x1, Pallas kernels: 76.9 us -> 65.6 us  [exchange(): pl.pallas_call(functools.partial(exchange_kernel, count, tile, split), ou...]
    all_to_all x1 -> x0, blocking collectives: 4.18 us -> none  [local(): lax.all_to_all(arranged, 'row', split_axis=0, concat_axis=2, tiled=True)]
    ppermute x2 -> x7, starting transfers between devices: 2.08 us -> 5.68 us  [the longest x1 1.57 us: local(): lax.ppermute(to_right[:, :tok], 'col', onward)]
    squeeze x1 -> x0, local copies, waits for them, and re-layouts: 1.17 us -> none  [local(): from_left = lax.ppermute(sums[0], 'col', onward)]
    unnamed x7 -> x11, local copies, waits for them, and re-layouts: 3.82 us -> 3.74 us
  transfers between devices with their start and end apart: 2 -> 7, of which waited for: 0 -> 0; matrix products, arithmetic and copies ran while one was open for 17% -> 0% of each run, Pallas kernels for 0% -> 21%
where the time goes in v2:
time: 97.2 us; the launch traced here: 96.9 us
  Pallas kernels  86.3 us (89%)
  starting transfers between devices  5.68 us (6%)
  local copies, waits for them, and re-layouts  3.8 us (4%)
    pallas_call x1, Pallas kernels, exchange(): pl.pallas_call(functools.partial(exchange_kernel, count, tile, split), ou...  65.6 us
    pallas_call x2, Pallas kernels, gradient_rows(): pl.pallas_call(gradient_kernel, grid=(blocks,), out_shape=jax.ShapeDtypeS...  20.6 us
    unnamed x11, local copies, waits for them, and re-layouts  3.74 us
  transfers between devices with their start and end apart: 7, of which 0 were waited for; matrix products, arithmetic and copies ran while one was open for 0% of the time, Pallas kernels for 21%

profile of v2, /device:TPU:0, one launch (start us, length us, event | category | flops | bytes accessed | tf_op | source)
XLA Modules:
  0.0 96.9 jit_solution(10253863716683711620)
XLA Ops:
  0.6 1.8 %copy.10 = bf16[128,2,768]{2,0,1:T(8,128)(2,1)} copy(bf16[128,2,768]{2,1,0:T(2,128)(2,1)} %param.3) | data formatting | bytes 786432 | tf_op args[0]
  2.4 65.6 %shard_map.58 = (bf16[128,3072]{1,0:T(8,128)(2,1)}, bf16[256,6144]{1,0:T(8,128)(2,1)}, bf16[256,3072]{1,0:T(8,128)(2,1)}, bf16[768,256]{1,0:T(8,128)(2,1)}, bf16...) custom-call(bf16[2,128,768]{2,1,0:T(8,128)(2,1)} %bitcast.9, ...), custom_call_target="tpu_custom_call" | custom-call | flops 19327352832 | bytes 37748736 | tf_op jit(solution)/shard_map/pallas_call | solution.py:281
  68.1 0.0 copy-start.2
  68.1 0.0 copy-start.1
  68.1 0.6 collective-permute-start
  68.7 1.5 %collective-permute-start.2 = (bf16[768,256]{1,0:T(8,128)(2,1)}, bf16[768,256]{1,0:T(8,128)(2,1)S(1)}, u32[]{:S(2)}, u32[]{:S(2)}) collective-permute-start(bf16[768,256]{1,0:T(8,128)(2,1)} %get-tuple-element.17), channel_id=1, source_target_pairs={{2,0},{4,2},{6,4},{7,6},{5,7},{3,5},{1,3},{0,1},{10,8},{12,10},{14... | collective-permute-start | bytes 1179656 | tf_op jit(solution)/shard_map/ppermute | solution.py:384
  70.2 0.0 collective-permute-start.4
  70.2 10.3 %shard_map.59.rest_0_ = bf16[6144,3072]{1,0:T(8,128)(2,1)} custom-call(bf16[256,6144]{1,0:T(8,128)(2,1)} %get-tuple-element.19.own_ref, bf16[256,3072]{1,0:T(8,128)(2,1)} %get-tuple-element.20.grad_ref), custom_call_target="tpu_custom_call" | custom-call | flops 4831838208 | bytes 22020096 | tf_op jit(solution)/shard_map/pallas_call | solution.py:350
  80.5 0.0 collective-permute-done
  80.5 0.0 copy-done.2
  80.5 0.1 add_convert_fusion.1
  80.6 0.7 collective-permute-start.5
  81.3 1.6 %collective-permute-start.1 = (bf16[768,128]{1,0:T(8,128)(2,1)S(1)}, bf16[768,128]{1,0:T(8,128)(2,1)S(1)}, u32[]{:S(2)}, u32[]{:S(2)}) collective-permute-start(bf16[768,128]{1,0:T(8,128)(2,1)S(1)} %get-tuple-element.28), channel_id=1, source_target_pairs={{0,2},{2,4},{4,6},{6,7},{7,5},{5,3},{3,1},{1,0},{8,10},{10,12},{12... | collective-permute-start | bytes 589832 | tf_op jit(solution)/shard_map/ppermute | solution.py:391
  82.9 0.0 collective-permute-done.2
  82.9 0.0 copy-done.1
  82.9 0.1 add_convert_fusion
  83.0 0.1 collective-permute-start.6
  83.1 0.0 copy-start.3
  83.1 0.0 copy-start
  83.1 1.2 %collective-permute-start.3 = (bf16[768,128]{1,0:T(8,128)(2,1)S(1)}, bf16[768,128]{1,0:T(8,128)(2,1)S(1)}, u32[]{:S(2)}, u32[]{:S(2)}) collective-permute-start(bf16[768,128]{1,0:T(8,128)(2,1)S(1)} %get-tuple-element.30), channel_id=1, source_target_pairs={{2,0},{4,2},{6,4},{7,6},{5,7},{3,5},{1,3},{0,1},{10,8},{12,10},{14... | collective-permute-start | bytes 589832 | tf_op jit(solution)/shard_map/ppermute | solution.py:392
  84.4 10.3 %shard_map.60 = bf16[6144,3072]{1,0:T(8,128)(2,1)} custom-call(bf16[256,6144]{1,0:T(8,128)(2,1)} %get-tuple-element.19.own_ref, bf16[256,3072]{1,0:T(8,128)(2,1)} %get-tuple-element.20.grad_ref, bf16[6144,3072]{1,0:T(8,128)(2,1)} %shard_map.59.rest_0_), custom_call_target="tpu_custom_call", output_to_operand_aliasing={{}: (2, {})} | custom-call | flops 4831838208 | bytes 22020096 | tf_op jit(solution)/shard_map/pallas_call | solution.py:350
  94.7 0.0 collective-permute-done.4
  94.7 0.0 collective-permute-done.5
  94.7 0.0 collective-permute-done.1
  94.7 0.0 collective-permute-done.6
  94.7 0.0 collective-permute-done.3
  94.7 0.0 copy-done.3
  94.7 0.2 select_bitcast_fusion.1
  95.0 1.1 %copy.8 = bf16[128,2,768]{2,1,0:T(2,128)(2,1)} copy(bf16[128,2,768]{0,2,1:T(8,128)(2,1)S(1)} %maximum_bitcast_fusion) | data formatting | bytes 786432
  96.0 0.0 copy-done
  96.0 0.9 copy.13
  (4 shorter events, 0.1 us)
Async XLA Ops:
  68.1 12.4 %copy-start.2 = (f32[768,256]{1,0:T(8,128)S(1)}, f32[768,256]{1,0:T(8,128)}, u32[]{:S(2)}) copy-start(f32[768,256]{1,0:T(8,128)} %get-tuple-element.14) | copy-start | bytes 2359300
  68.1 14.8 %copy-start.1 = (f32[768,256]{1,0:T(8,128)S(1)}, f32[768,256]{1,0:T(8,128)}, u32[]{:S(2)}) copy-start(f32[768,256]{1,0:T(8,128)} %get-tuple-element.16) | copy-start | bytes 2359300
  68.1 12.4 %collective-permute-start = (bf16[768,256]{1,0:T(8,128)(2,1)}, bf16[768,256]{1,0:T(8,128)(2,1)S(1)}, u32[]{:S(2)}, u32[]{:S(2)}) collective-permute-start(bf16[768,256]{1,0:T(8,128)(2,1)} %get-tuple-element.15), channel_id=1, source_target_pairs={{0,2},{2,4},{4,6},{6,7},{7,5},{5,3},{3,1},{1,0},{8,10},{10,12},{12... | collective-permute-start | bytes 1179656 | tf_op jit(solution)/shard_map/ppermute | solution.py:383
  68.7 14.2 %collective-permute-start.2 = (bf16[768,256]{1,0:T(8,128)(2,1)}, bf16[768,256]{1,0:T(8,128)(2,1)S(1)}, u32[]{:S(2)}, u32[]{:S(2)}) collective-permute-start(bf16[768,256]{1,0:T(8,128)(2,1)} %get-tuple-element.17), channel_id=1, source_target_pairs={{2,0},{4,2},{6,4},{7,6},{5,7},{3,5},{1,3},{0,1},{10,8},{12,10},{14... | collective-permute-start | bytes 1179656 | tf_op jit(solution)/shard_map/ppermute | solution.py:384
  70.2 24.5 %collective-permute-start.4 = (f32[768,128]{1,0:T(8,128)}, f32[768,128]{1,0:T(8,128)S(1)}, u32[]{:S(2)}, u32[]{:S(2)}) collective-permute-start(f32[768,128]{1,0:T(8,128)} %get-tuple-element.18), channel_id=1, source_target_pairs={{0,8},{8,0},{1,9},{9,1},{2,10},{10,2},{3,11},{11,3},{4,12},{12,4},... | collective-permute-start | bytes 1179656 | tf_op jit(solution)/shard_map/ppermute | solution.py:385
  80.6 14.1 %collective-permute-start.5 = (bf16[768,128]{1,0:T(8,128)(2,1)S(1)}, bf16[768,128]{1,0:T(8,128)(2,1)S(1)}, u32[]{:S(2)}, u32[]{:S(2)}) collective-permute-start(bf16[768,128]{1,0:T(8,128)(2,1)S(1)} %get-tuple-element.27), channel_id=1, source_target_pairs={{0,10},{2,12},{4,14},{6,15},{7,13},{5,11},{3,9},{1,8},{8,2},{10,4}... | collective-permute-start | bytes 589832 | tf_op jit(solution)/shard_map/ppermute | solution.py:395
  81.3 13.3 %collective-permute-start.1 = (bf16[768,128]{1,0:T(8,128)(2,1)S(1)}, bf16[768,128]{1,0:T(8,128)(2,1)S(1)}, u32[]{:S(2)}, u32[]{:S(2)}) collective-permute-start(bf16[768,128]{1,0:T(8,128)(2,1)S(1)} %get-tuple-element.28), channel_id=1, source_target_pairs={{0,2},{2,4},{4,6},{6,7},{7,5},{5,3},{3,1},{1,0},{8,10},{10,12},{12... | collective-permute-start | bytes 589832 | tf_op jit(solution)/shard_map/ppermute | solution.py:391
  83.0 11.7 %collective-permute-start.6 = (bf16[768,128]{1,0:T(8,128)(2,1)S(1)}, bf16[768,128]{1,0:T(8,128)(2,1)S(1)}, u32[]{:S(2)}, u32[]{:S(2)}) collective-permute-start(bf16[768,128]{1,0:T(8,128)(2,1)S(1)} %get-tuple-element.29), channel_id=1, source_target_pairs={{2,8},{4,10},{6,12},{7,14},{5,15},{3,13},{1,11},{0,9},{10,0},{12,2... | collective-permute-start | bytes 589832 | tf_op jit(solution)/shard_map/ppermute | solution.py:396
  83.1 11.6 %copy-start.3 = (f32[768,128]{1,0:T(8,128)S(1)}, f32[768,128]{1,0:T(8,128)}, u32[]{:S(2)}) copy-start(f32[768,128]{1,0:T(8,128)} %get-tuple-element.13) | copy-start | bytes 1179652
  83.1 12.9 %copy-start = (bf16[128,3072]{1,0:T(8,128)(2,1)S(1)}, bf16[128,3072]{1,0:T(8,128)(2,1)}, u32[]{:S(2)}) copy-start(bf16[128,3072]{1,0:T(8,128)(2,1)} %get-tuple-element.34) | copy-start | bytes 2359300
  83.1 11.6 %collective-permute-start.3 = (bf16[768,128]{1,0:T(8,128)(2,1)S(1)}, bf16[768,128]{1,0:T(8,128)(2,1)S(1)}, u32[]{:S(2)}, u32[]{:S(2)}) collective-permute-start(bf16[768,128]{1,0:T(8,128)(2,1)S(1)} %get-tuple-element.30), channel_id=1, source_target_pairs={{2,0},{4,2},{6,4},{7,6},{5,7},{3,5},{1,3},{0,1},{10,8},{12,10},{14... | collective-permute-start | bytes 589832 | tf_op jit(solution)/shard_map/ppermute | solution.py:392
